TPU v7x, 512 devices: a whole 4x8x8 slice. The times are simulated.
512 devices in a mesh: dp: 64 (over z, x, y_hi), tensor: 8 (over y_lo, core).
Axes of the slice: x: 4, y: 8 (y_hi: 2, y_lo: 4; y = y_hi * 4 + y_lo), z: 8, core: 2. Of those that a mesh axis runs over, the one named last changes fastest.
Arguments:
- activations: bfloat16 [65536, 8192], P(('dp', 'tensor')), may hold values from -64 to 64
- out_grads: bfloat16 [65536, 10240], P('dp', 'tensor'), may hold values from -64 to 64
- act_old: float32 [16, 512, 512], P('tensor', 'dp'), may hold values from -20 to 44, as said below
- grad_old: float32 [40, 256, 256], P('tensor', 'dp'), may hold values from -20 to 44, as said below
Outputs:
- act_new: float32 [16, 512, 512], P('tensor', 'dp')
- grad_new: float32 [40, 256, 256], P('tensor', 'dp')
Inputs may be any that keep to these rules, and one draw needn't show every extreme that they name: `act_old`: each block is symmetric. `grad_old`: each block is symmetric.
All inputs are finite; a program needn't handle non-finite values.
Results may differ from a plain program's by a relative error of at most 0.0003.
Values may be sent and summed in bfloat16 or wider, within the bound.
A program may use at most 64 MiB of HBM per device.

v0:
```python
import jax
import jax.numpy as jnp
from jax import lax
from jax.sharding import PartitionSpec as P

ABLK = 512
GBLK = 256


DECAY_RATE = 0.5


def block_products(matrix, block_width):
    row_count = matrix.shape[0]
    blocked = matrix.reshape(row_count, matrix.shape[1] // block_width, block_width)
    return jnp.einsum("tbi,tbj->bij", blocked, blocked, preferred_element_type=jnp.float32)


def activation_partials(activations):
    col_tokens = lax.all_to_all(activations, "tensor", split_axis=1, concat_axis=0, tiled=True)
    return block_products(col_tokens, ABLK)


def on_device(activations, out_grads, act_old, grad_old):
    total_rows = out_grads.shape[0] * lax.axis_size("dp")
    norm_scale = (1.0 - DECAY_RATE) / total_rows
    grad_part = block_products(out_grads, GBLK)
    act_part = activation_partials(activations)
    act_sum, grad_sum = (
        lax.psum_scatter(act_part, "dp", scatter_dimension=1, tiled=True),
        lax.psum_scatter(grad_part, "dp", scatter_dimension=1, tiled=True),
    )
    act_new = DECAY_RATE * act_old + norm_scale * act_sum
    grad_new = DECAY_RATE * grad_old + norm_scale * grad_sum
    return (act_new, grad_new)


def solution(mesh):
    return jax.shard_map(
        on_device,
        mesh=mesh,
        in_specs=(
            P(("dp", "tensor"), None),
            P("dp", "tensor"),
            P("tensor", "dp", None),
            P("tensor", "dp", None),
        ),
        out_specs=(P("tensor", "dp", None), P("tensor", "dp", None)),
        check_vma=False,
    )
```

profile of v0, /device:TPU:6, one launch (start us, length us, event | category | flops | bytes accessed | tf_op | source)
XLA Modules:
  0.0 1305.2 jit_solution(7147180066306334443)
XLA Ops:
  7.2 4.1 copy.13
  11.2 4.9 all-to-all-start
  16.1 0.0 all-reduce.3.cloned.1.call-start
  16.2 3.0 copy.16
  19.2 2.0 fusion.2
  21.2 0.0 all-reduce.3.cloned.1.call-update
  21.2 0.0 reduce-scatter.3.cloned.1.call-start
  21.2 49.2 %all-to-all-done = bf16[128,8,1024]{0,2,1:T(8,128)(2,1)} async-done(((bf16[128,8,1024]{0,2,1:T(8,128)(2,1)}), bf16[128,8,1024]{0,2,1:T(8,128)(2,1)}, u32[]{:S(2)}, u32[]{:S(2)}) %all-to-all-start) | async-done | bytes 2097184 | tf_op jit(solution)/shard_map/all_to_all | solution.py:20
  70.4 2.9 copy.14
  73.4 2.3 reshape.14
  75.7 4.8 fusion.1
  80.5 0.0 copy-start.1
  80.5 0.0 copy-start
  80.5 0.0 reduce-scatter.3.cloned.1.call-update
  80.5 1.3 dynamic-slice
  82.5 781.3 %all-reduce.3.cloned.1.call-done = f32[5,256,256]{2,1,0:T(8,128)} async-done(((f32[5,256,256]{2,1,0:T(8,128)}), f32[5,256,256]{2,1,0:T(8,128)}) %all-reduce.3.cloned.1.call-update) | async-done | bytes 1310736
  863.8 0.0 copy-done.1
  863.8 1.4 fusion
  865.2 431.8 %reduce-scatter.3.cloned.1.call-done = f32[2,8,512]{2,1,0:T(8,128)} async-done(((f32[2,512,512]{2,1,0:T(8,128)}), f32[2,8,512]{2,1,0:T(8,128)}) %reduce-scatter.3.cloned.1.call-update) | async-done | bytes 32784 | tf_op jit(solution)/shard_map/reduce_scatter | solution.py:30
  1296.9 0.0 copy-done
  1297.0 1.4 multiply_add_fusion
Async XLA Ops:
  11.2 59.2 %all-to-all-start = ((bf16[128,8,1024]{0,2,1:T(8,128)(2,1)}), bf16[128,8,1024]{0,2,1:T(8,128)(2,1)}, u32[]{:S(2)}, u32[]{:S(2)}) async-start(bf16[128,8,1024]{0,2,1:T(8,128)(2,1)} %bitcast), calls=%async_computation | async-start | bytes 4194304 | tf_op jit(solution)/shard_map/all_to_all | solution.py:20
  16.1 847.7 %all-reduce.3.cloned.1.call-start = ((), (), s32[]{:S(2)}) async-start(), calls=%async_computation.3 | async-start | bytes 2621440
  21.2 1275.8 %reduce-scatter.3.cloned.1.call-start = ((), (), s32[]{:S(2)}) async-start(), calls=%async_computation.2 | async-start | bytes 2129920 | tf_op jit(solution)/shard_map/reduce_scatter | solution.py:30
  80.5 783.3 %copy-start.1 = (f32[5,4,256]{2,1,0:T(4,128)S(1)}, f32[5,4,256]{2,1,0:T(4,128)}, u32[]{:S(2)}) copy-start(f32[5,4,256]{2,1,0:T(4,128)} %param.7) | copy-start | bytes 61444
  80.5 1216.4 %copy-start = (f32[2,8,512]{2,1,0:T(8,128)S(1)}, f32[2,8,512]{2,1,0:T(8,128)}, u32[]{:S(2)}) copy-start(f32[2,8,512]{2,1,0:T(8,128)} %param.6) | copy-start | bytes 98308
Sparse Core Ops, SparseCore 0:
  21.3 842.4 all-reduce.2
  866.8 430.1 reduce-scatter.2
where the time goes:
time: 1320 us; the launch traced here: 1310 us
  waiting for transfers between devices  1260 us (95%)
  between operations  14.7 us (1%)
  local copies, waits for them, and re-layouts  13.6 us (1%)
    unnamed x3, waiting for transfers between devices  781 us
    reduce_scatter x1, waiting for transfers between devices, on_device(): lax.psum_scatter(act_part, 'dp', scatter_dimension=1, tiled=True)  432 us
    all_to_all x1, waiting for transfers between devices, activation_partials(): lax.all_to_all(activations, 'tensor', split_axis=1, concat_axis=0, tiled=...  49.2 us
  transfers between devices with their start and end apart: 3, of which 3 were waited for; matrix products, arithmetic and copies ran while one was open for 1% of the time, Pallas kernels for 0%

commit v1 on v0

v1 whole, which is shorter than its diff:
```python
import functools

import jax
import jax.numpy as jnp
from jax import lax
from jax.experimental import pallas as pl
from jax.experimental.pallas import tpu as pltpu
from jax.sharding import PartitionSpec as P

MESH = pl.DeviceIdType.MESH
F32 = jnp.float32
BF16 = jnp.bfloat16
DECAY_RATE = 0.5

FIRST = BF16
X, Y, Z = 0, 1, 2
ORDERS = ((X, Y, Z), (X, Z, Y), (Y, X, Z), (Z, X, Y))


def gram(left, right):
    return lax.dot_general(left, right, (((0,), (0,)), ((), ())), preferred_element_type=F32)


def kernel(
    act_ref, grad_ref, act_out, grad_out,
    gv, xo, xc, xy, xz, xd, acc,
    a_own, a_snd, a_r1, a_s2, a_r2, a_s3, a_r3, fin, fin_r,
    g_own, g_snd, g_r1, g_s2, g_r2, g_s3, g_r3,
    local_sem, tok_send, tok_recv, a_send, a_recv, fin_sem, g_send, g_recv,
):
    dp = lax.axis_index("dp")
    tensor = lax.axis_index("tensor")
    yh = dp % 2
    x = (dp // 2) % 4
    z = dp // 8
    c = tensor % 2
    y = yh * 4 + tensor // 2
    yp, zp = y % 2, z % 2
    q, m = y // 2, z // 2

    def device(zz, xx, yy, cc):
        return ((zz * 4 + xx) * 2 + yy // 4, (yy % 4) * 2 + cc)

    def columns(half, ypar, core, zpar):
        return pl.ds(pl.multiple_of((half * 8 + ypar * 4 + core * 2 + zpar) * 512, 512), 512)

    def send(src, dst, send_sem, recv_sem, target):
        pltpu.make_async_remote_copy(
            src_ref=src, dst_ref=dst, send_sem=send_sem, recv_sem=recv_sem,
            device_id=target, device_id_type=MESH,
        ).start()

    here = (dp, tensor)

    def arrived(buf, sem):
        pltpu.make_async_remote_copy(
            src_ref=buf, dst_ref=buf, send_sem=sem, recv_sem=sem,
            device_id=here, device_id_type=MESH,
        ).wait_recv()

    def left(buf, sem):
        pltpu.make_async_remote_copy(
            src_ref=buf, dst_ref=buf, send_sem=sem, recv_sem=sem,
            device_id=here, device_id_type=MESH,
        ).wait_send()

    grads_in = pltpu.make_async_copy(grad_ref, gv, local_sem.at[0])
    grads_in.start()
    own_in = [
        pltpu.make_async_copy(act_ref.at[:, columns(h, yp, c, zp)], xo.at[h], local_sem.at[1 + h])
        for h in range(2)
    ]
    for copy in own_in:
        copy.start()

    yn = ((y + 1) % 8, (y + 7) % 8)
    zn = ((z + 1) % 8, (z + 7) % 8)
    cores = (c, 1 - c)
    oy, oz = 1 - yp, 1 - zp

    peers = [device(z, x, y, 1 - c)]
    peers += [device(z, x, yn[s], cores[f]) for s in range(2) for f in range(2)]
    peers += [device(zn[s], x, y, cores[f]) for s in range(2) for f in range(2)]
    peers += [device(zn[t], x, yn[s], cores[f]) for s in range(2) for t in range(2) for f in range(2)]
    peers += [device(z, (x + k) % 4, y, c) for k in range(1, 4)]
    peers += [device(z, x, (y + 2 * k) % 8, c) for k in range(1, 4)]
    peers += [device((z + k) % 8, x, y, c) for k in range(2, 7)]
    barrier = pltpu.get_barrier_semaphore()
    for peer in peers:
        pl.semaphore_signal(barrier, inc=1, device_id=peer, device_id_type=MESH)
    pl.semaphore_wait(barrier, len(peers))

    for s in range(2):
        for t in range(2):
            for f in range(2):
                n = s * 2 + t
                for h in range(2):
                    send(
                        act_ref.at[pl.ds(n * 32, 32), columns(h, oy, cores[f], oz)],
                        xd.at[h, pl.ds((n * 2 + f) * 32, 32)],
                        tok_send.at[3], tok_recv.at[3], device(zn[t], x, yn[s], cores[f]),
                    )
    for s in range(2):
        for f in range(2):
            for h in range(2):
                send(
                    act_ref.at[pl.ds(s * 64, 64), columns(h, oy, cores[f], zp)],
                    xy.at[h, pl.ds((s * 2 + f) * 64, 64)],
                    tok_send.at[1], tok_recv.at[1], device(z, x, yn[s], cores[f]),
                )
                send(
                    act_ref.at[pl.ds(s * 64, 64), columns(h, yp, cores[f], oz)],
                    xz.at[h, pl.ds((s * 2 + f) * 64, 64)],
                    tok_send.at[2], tok_recv.at[2], device(zn[s], x, y, cores[f]),
                )
    for h in range(2):
        send(
            act_ref.at[:, columns(h, yp, 1 - c, zp)], xc.at[h],
            tok_send.at[0], tok_recv.at[0], device(z, x, y, 1 - c),
        )

    grads_in.wait()
    for b in range(5):
        block = gv[:, b * 256:(b + 1) * 256]
        part = gram(block, block)
        for xx in range(4):
            for mm in range(4):
                r = mm * 64 + xx * 8
                rows = jnp.concatenate([part[r:r + 8], part[r + 32:r + 40]], axis=0)
                g_own[xx, mm, b] = rows
                g_snd[xx, mm, b] = rows.astype(FIRST)
    for k in range(1, 4):
        to = (x + k) % 4
        send(g_snd.at[to], g_r1.at[k - 1], g_send.at[0], g_recv.at[0], device(z, to, y, c))

    for copy in own_in:
        copy.wait()
    for h in range(2):
        for i in range(2):
            acc[h, i * 256:(i + 1) * 256] = gram(xo[h, :, i * 256:(i + 1) * 256], xo[h])
    for buf, g in ((xc, 0), (xy, 1), (xz, 2)):
        arrived(buf, tok_recv.at[g])
        for h in range(2):
            for i in range(2):
                acc[h, i * 256:(i + 1) * 256] += gram(buf[h, :, i * 256:(i + 1) * 256], buf[h])
    arrived(xd, tok_recv.at[3])
    for h in range(2):
        for mm in range(4):
            part = acc[h, mm * 128:(mm + 1) * 128] + gram(xd[h, :, mm * 128:(mm + 1) * 128], xd[h])
            for xx in range(4):
                for hi in range(2):
                    r = xx * 16 + hi * 8
                    rows = jnp.concatenate([part[r:r + 8], part[r + 64:r + 72]], axis=0)
                    at = (xx, hi * 2 + h, mm)
                    for p in range(4):
                        i1, i2, i3 = (at[axis] for axis in ORDERS[p])
                        piece = rows[:, p * 128:(p + 1) * 128]
                        a_own[p, i1, i2, i3] = piece
                        a_snd[p, i1, i2, i3] = piece.astype(FIRST)

    me = (x, q, m)

    def scatter(src, dst, axis, send_sem, recv_sem):
        for k in (2, 1, 3):
            to = (me[axis] + k) % 4
            target = (
                device(z, to, y, c) if axis == X
                else device(z, x, (y + 2 * k) % 8, c) if axis == Y
                else device((z + 2 * k) % 8, x, y, c)
            )
            send(src.at[to], dst.at[k - 1], send_sem, recv_sem, target)

    for p in (2, 3, 0, 1):
        scatter(a_snd.at[p], a_r1.at[p], ORDERS[p][0], a_send.at[p, 0], a_recv.at[p, 0])

    arrived(g_r1, g_recv.at[0])
    for mm in range(4):
        for b in range(5):
            rows = g_own[x, mm, b]
            for k in range(3):
                rows += g_r1[k, mm, b].astype(F32)
            g_s2[2 * mm, b] = rows[:8]
            g_s2[2 * mm + 1, b] = rows[8:]
    for k in (4, 3, 5, 2, 6, 1, 7):
        to = (z + k) % 8
        send(g_s2.at[to], g_r2.at[k - 1], g_send.at[1], g_recv.at[1], device(to, x, y, c))

    for p in range(4):
        arrived(a_r1.at[p], a_recv.at[p, 0])
        own = me[ORDERS[p][0]]
        total = a_own[p, own]
        for k in range(3):
            total += a_r1[p, k].astype(F32)
        a_s2[p] = total
        scatter(a_s2.at[p], a_r2.at[p], ORDERS[p][1], a_send.at[p, 1], a_recv.at[p, 1])

    arrived(g_r2, g_recv.at[1])
    rest = g_s2[z]
    for k in range(7):
        rest += g_r2[k]
    g_s3[...] = rest
    send(g_s3, g_r3, g_send.at[2], g_recv.at[2], device(z, x, (y + 4) % 8, c))

    for p in range(4):
        arrived(a_r2.at[p], a_recv.at[p, 1])
        own = me[ORDERS[p][1]]
        total = a_s2[p, own]
        for k in range(3):
            total += a_r2[p, k]
        a_s3[p] = total
        scatter(a_s3.at[p], a_r3.at[p], ORDERS[p][2], a_send.at[p, 2], a_recv.at[p, 2])

    for p in range(4):
        arrived(a_r3.at[p], a_recv.at[p, 2])
        own = me[ORDERS[p][2]]
        total = a_s3[p, own]
        for k in range(3):
            total += a_r3[p, k]
        fin[0, :, p * 128:(p + 1) * 128] = total[:8]
        fin[1, :, p * 128:(p + 1) * 128] = total[8:]
    partner = device(z + 1 - 2 * zp, x, y, c)
    send(fin.at[oz], fin_r, fin_sem.at[0], fin_sem.at[1], partner)
    arrived(g_r3, g_recv.at[2])
    grad_out[...] = g_s3[...] + g_r3[...]
    act_out[zp] = fin[zp]
    arrived(fin_r, fin_sem.at[1])
    act_out[oz] = fin_r[...]

    for buf, g in ((xc, 0), (xy, 1), (xz, 2), (xd, 3)):
        left(buf, tok_send.at[g])
    for p in range(4):
        left(a_r1.at[p], a_send.at[p, 0])
        left(a_r2.at[p], a_send.at[p, 1])
        left(a_r3.at[p], a_send.at[p, 2])
    left(g_r1, g_send.at[0])
    left(g_r2, g_send.at[1])
    left(g_r3, g_send.at[2])
    left(fin_r, fin_sem.at[0])


def statistics(activations, out_grads):
    any_spec = pl.BlockSpec(memory_space=pl.ANY)
    vmem_spec = pl.BlockSpec(memory_space=pltpu.VMEM)
    vmem = pltpu.VMEM
    dma = pltpu.SemaphoreType.DMA
    return pl.pallas_call(
        kernel,
        out_shape=(jax.ShapeDtypeStruct((2, 8, 512), F32), jax.ShapeDtypeStruct((5, 8, 256), F32)),
        in_specs=[any_spec, any_spec],
        out_specs=(vmem_spec, vmem_spec),
        scratch_shapes=[
            vmem((1024, 1280), BF16),
            vmem((2, 128, 512), BF16),
            vmem((2, 128, 512), BF16),
            vmem((2, 256, 512), BF16),
            vmem((2, 256, 512), BF16),
            vmem((2, 256, 512), BF16),
            vmem((2, 512, 512), F32),
            vmem((4, 4, 4, 4, 16, 128), F32),
            vmem((4, 4, 4, 4, 16, 128), FIRST),
            vmem((4, 3, 4, 4, 16, 128), FIRST),
            vmem((4, 4, 4, 16, 128), F32),
            vmem((4, 3, 4, 16, 128), F32),
            vmem((4, 4, 16, 128), F32),
            vmem((4, 3, 16, 128), F32),
            vmem((2, 8, 512), F32),
            vmem((8, 512), F32),
            vmem((4, 4, 5, 16, 256), F32),
            vmem((4, 4, 5, 16, 256), FIRST),
            vmem((3, 4, 5, 16, 256), FIRST),
            vmem((8, 5, 8, 256), F32),
            vmem((7, 5, 8, 256), F32),
            vmem((5, 8, 256), F32),
            vmem((5, 8, 256), F32),
            dma((3,)),
            dma((4,)),
            dma((4,)),
            dma((4, 3)),
            dma((4, 3)),
            dma((2,)),
            dma((3,)),
            dma((3,)),
        ],
        compiler_params=pltpu.CompilerParams(
            collective_id=0, has_side_effects=True, vmem_limit_bytes=40 * 1024 * 1024
        ),
        cost_estimate=pl.CostEstimate(flops=1_800_000_000, bytes_accessed=5_000_000, transcendentals=0),
    )(activations, out_grads)


def on_device(activations, out_grads, act_old, grad_old):
    total_rows = out_grads.shape[0] * lax.axis_size("dp")
    norm_scale = (1.0 - DECAY_RATE) / total_rows
    act_sum, grad_rows = statistics(activations, out_grads)
    first = (lax.axis_index("dp") % 2) * 4
    grad_sum = lax.dynamic_slice_in_dim(grad_rows, first, 4, 1)
    act_new = DECAY_RATE * act_old + norm_scale * act_sum
    grad_new = DECAY_RATE * grad_old + norm_scale * grad_sum
    return (act_new, grad_new)


def solution(mesh):
    return jax.shard_map(
        on_device,
        mesh=mesh,
        in_specs=(
            P(("dp", "tensor"), None),
            P("dp", "tensor"),
            P("tensor", "dp", None),
            P("tensor", "dp", None),
        ),
        out_specs=(P("tensor", "dp", None), P("tensor", "dp", None)),
        check_vma=False,
    )
```

time: 1320 us -> 60.7 us (0.05); the launches traced: 1310 us -> 60.4 us
  waiting for transfers between devices: 1260 us -> 0 us
  Pallas kernels: 0 us -> 55.2 us
  between operations: 14.7 us -> 0.67 us
    unnamed x3 -> x0, waiting for transfers between devices: 781 us -> none
    reduce_scatter x1 -> x0, waiting for transfers between devices: 432 us -> none  [on_device(): lax.psum_scatter(act_part, 'dp', scatter_dimension=1, tiled=True)]
    pallas_call x0 -> x1, Pallas kernels: none -> 55.2 us  [statistics(): pl.pallas_call(kernel, out_shape=(jax.ShapeDtypeStruct((2, 8, 512), F32),...]
    all_to_all x1 -> x0, waiting for transfers between devices: 49.2 us -> none  [activation_partials(): lax.all_to_all(activations, 'tensor', split_axis=1, concat_axis=0, tiled=...]
  transfers between devices with their start and end apart: 3 -> 0, of which waited for: 3 -> 0; matrix products, arithmetic and copies ran while one was open for 1% -> 0% of each run, Pallas kernels for 0% -> 0%
where the time goes in v1:
time: 60.7 us; the launch traced here: 60.4 us
  Pallas kernels  55.2 us (91%)
  local copies, waits for them, and re-layouts  3.33 us (5%)
  other arithmetic  1.25 us (2%)
  between operations  0.67 us (1%)
    pallas_call x1, Pallas kernels, statistics(): pl.pallas_call(kernel, out_shape=(jax.ShapeDtypeStruct((2, 8, 512), F32),...  55.2 us
    unnamed x8, local copies, waits for them, and re-layouts  3.33 us

profile of v1, /device:TPU:6, one launch (start us, length us, event | category | flops | bytes accessed | tf_op | source)
XLA Modules:
  0.0 60.4 jit_solution(7355913627502324215)
XLA Ops:
  0.6 0.0 copy-start
  0.7 1.7 %copy-done = bf16[1024,1280]{1,0:T(8,128)(2,1)S(1)} copy-done((bf16[1024,1280]{1,0:T(8,128)(2,1)S(1)}, bf16[1024,1280]{1,0:T(8,128)(2,1)}, u32[]{:S(2)}) %copy-start) | copy-done | bytes 2621464
  2.4 0.0 copy-start.1
  2.4 1.6 %copy-done.1 = bf16[128,8192]{1,0:T(8,128)(2,1)S(1)} copy-done((bf16[128,8192]{1,0:T(8,128)(2,1)S(1)}, bf16[128,8192]{1,0:T(8,128)(2,1)}, u32[]{:S(2)}) %copy-start.1) | copy-done | bytes 2097176
  4.0 0.0 copy-start.3
  4.0 0.0 copy-start.2
  4.0 55.2 %shard_map.59 = (f32[2,8,512]{2,1,0:T(8,128)S(1)}, f32[5,8,256]{2,1,0:T(8,128)S(1)}) custom-call(bf16[128,8192]{1,0:T(8,128)(2,1)S(1)} %copy-done.1, bf16[1024,1280]{1,0:T(8,128)(2,1)S(1)} %copy-done), custom_call_target="tpu_custom_call" | custom-call | flops 1800000000 | bytes 5000000 | tf_op jit(solution)/shard_map/pallas_call | solution.py:246
  59.2 0.0 copy-done.3
  59.2 0.6 %multiply_add_fusion.1 = f32[5,4,256]{2,1,0:T(4,128)} fusion(f32[5,8,256]{2,1,0:T(8,128)S(1)} %get-tuple-element.5, s32[]{:T(128)S(6)} %select_n.11, f32[5,4,256]{2,1,0:T(4,128)S(1)} %copy-done.3), kind=kLoop, calls=%fused_computation.1 | loop fusion | flops 15360 | bytes 61444 | tf_op jit(solution)/shard_map/add | solution.py:298
  59.8 0.0 copy-done.2
  59.8 0.6 %multiply_add_fusion = f32[2,8,512]{2,1,0:T(8,128)} fusion(f32[2,8,512]{2,1,0:T(8,128)S(1)} %get-tuple-element.4, f32[2,8,512]{2,1,0:T(8,128)S(1)} %copy-done.2), kind=kLoop, calls=%fused_computation | loop fusion | flops 24576 | bytes 98304 | tf_op jit(solution)/shard_map/add | solution.py:297
Async XLA Ops:
  0.6 1.7 %copy-start = (bf16[1024,1280]{1,0:T(8,128)(2,1)S(1)}, bf16[1024,1280]{1,0:T(8,128)(2,1)}, u32[]{:S(2)}) copy-start(bf16[1024,1280]{1,0:T(8,128)(2,1)} %grad_ref.1) | copy-start | bytes 7864324
  2.4 1.6 %copy-start.1 = (bf16[128,8192]{1,0:T(8,128)(2,1)S(1)}, bf16[128,8192]{1,0:T(8,128)(2,1)}, u32[]{:S(2)}) copy-start(bf16[128,8192]{1,0:T(8,128)(2,1)} %act_ref.1) | copy-start | bytes 6291460
  4.0 55.2 %copy-start.3 = (f32[5,4,256]{2,1,0:T(4,128)S(1)}, f32[5,4,256]{2,1,0:T(4,128)}, u32[]{:S(2)}) copy-start(f32[5,4,256]{2,1,0:T(4,128)} %param.7) | copy-start | bytes 61444
  4.0 55.8 %copy-start.2 = (f32[2,8,512]{2,1,0:T(8,128)S(1)}, f32[2,8,512]{2,1,0:T(8,128)}, u32[]{:S(2)}) copy-start(f32[2,8,512]{2,1,0:T(8,128)} %param.6) | copy-start | bytes 98308

commit v2 on v1

--- a/solution.py
+++ b/solution.py
@@ -133,12 +133,27 @@
         to = (x + k) % 4
         send(g_snd.at[to], g_r1.at[k - 1], g_send.at[0], g_recv.at[0], device(z, to, y, c))
 
+    def second_gradients():
+        arrived(g_r1, g_recv.at[0])
+        for mm in range(4):
+            for b in range(5):
+                rows = g_own[x, mm, b]
+                for k in range(3):
+                    rows += g_r1[k, mm, b].astype(F32)
+                g_s2[2 * mm, b] = rows[:8]
+                g_s2[2 * mm + 1, b] = rows[8:]
+        for k in (4, 3, 5, 2, 6, 1, 7):
+            to = (z + k) % 8
+            send(g_s2.at[to], g_r2.at[k - 1], g_send.at[1], g_recv.at[1], device(to, x, y, c))
+
     for copy in own_in:
         copy.wait()
     for h in range(2):
         for i in range(2):
             acc[h, i * 256:(i + 1) * 256] = gram(xo[h, :, i * 256:(i + 1) * 256], xo[h])
     for buf, g in ((xc, 0), (xy, 1), (xz, 2)):
+        if g == 1:
+            second_gradients()
         arrived(buf, tok_recv.at[g])
         for h in range(2):
             for i in range(2):
@@ -172,18 +187,6 @@
 
     for p in (2, 3, 0, 1):
         scatter(a_snd.at[p], a_r1.at[p], ORDERS[p][0], a_send.at[p, 0], a_recv.at[p, 0])
-
-    arrived(g_r1, g_recv.at[0])
-    for mm in range(4):
-        for b in range(5):
-            rows = g_own[x, mm, b]
-            for k in range(3):
-                rows += g_r1[k, mm, b].astype(F32)
-            g_s2[2 * mm, b] = rows[:8]
-            g_s2[2 * mm + 1, b] = rows[8:]
-    for k in (4, 3, 5, 2, 6, 1, 7):
-        to = (z + k) % 8
-        send(g_s2.at[to], g_r2.at[k - 1], g_send.at[1], g_recv.at[1], device(to, x, y, c))
 
     for p in range(4):
         arrived(a_r1.at[p], a_recv.at[p, 0])
@@ -282,7 +285,7 @@
             dma((3,)),
         ],
         compiler_params=pltpu.CompilerParams(
-            collective_id=0, has_side_effects=True, vmem_limit_bytes=40 * 1024 * 1024
+            collective_id=0, has_side_effects=True, vmem_limit_bytes=60 * 1024 * 1024
         ),
         cost_estimate=pl.CostEstimate(flops=1_800_000_000, bytes_accessed=5_000_000, transcendentals=0),
     )(activations, out_grads)

time: 60.7 us -> 58.1 us (0.957); the launches traced: 60.4 us -> 57.1 us
  local copies, waits for them, and re-layouts: 3.33 us -> 0.01 us
  Pallas kernels: 55.2 us -> 53.6 us
  other arithmetic: 1.25 us -> 2.78 us
    unnamed x8 -> x4, local copies, waits for them, and re-layouts: 3.33 us -> 0.01 us
    pallas_call x1, Pallas kernels: 55.2 us -> 53.6 us  [statistics(): pl.pallas_call(kernel, out_shape=(jax.ShapeDtypeStruct((2, 8, 512), F32),...]
    add x1, other arithmetic: 0.62 us -> 1.4 us  [on_device(): grad_new = DECAY_RATE * grad_old + norm_scale * grad_sum]
    add x1, other arithmetic: 0.62 us -> 1.38 us  [on_device(): act_new = DECAY_RATE * act_old + norm_scale * act_sum]
where the time goes in v2:
time: 58.1 us; the launch traced here: 57.1 us
  Pallas kernels  53.6 us (92%)
  other arithmetic  2.78 us (5%)
  between operations  0.68 us (1%)
    pallas_call x1, Pallas kernels, statistics(): pl.pallas_call(kernel, out_shape=(jax.ShapeDtypeStruct((2, 8, 512), F32),...  53.6 us
    add x1, other arithmetic, on_device(): grad_new = DECAY_RATE * grad_old + norm_scale * grad_sum  1.4 us
    add x1, other arithmetic, on_device(): act_new = DECAY_RATE * act_old + norm_scale * act_sum  1.38 us

profile of v2, /device:TPU:6, one launch (start us, length us, event | category | flops | bytes accessed | tf_op | source)
XLA Modules:
  0.0 57.1 jit_solution(8827512418214535437)
XLA Ops:
  0.6 0.0 copy-start.1
  0.7 0.0 copy-start
  0.7 53.6 %shard_map.59 = (f32[2,8,512]{2,1,0:T(8,128)}, f32[5,8,256]{2,1,0:T(8,128)}) custom-call(bf16[128,8192]{1,0:T(8,128)(2,1)} %act_ref.1, bf16[1024,1280]{1,0:T(8,128)(2,1)} %grad_ref.1), custom_call_target="tpu_custom_call" | custom-call | flops 1800000000 | bytes 5000000 | tf_op jit(solution)/shard_map/pallas_call | solution.py:249
  54.3 0.0 copy-done.1
  54.3 1.4 %multiply_add_fusion.1 = f32[5,4,256]{2,1,0:T(4,128)} fusion(f32[5,8,256]{2,1,0:T(8,128)} %get-tuple-element.5, s32[]{:T(128)S(6)} %select_n.11, f32[5,4,256]{2,1,0:T(4,128)S(1)} %copy-done.1), kind=kLoop, calls=%fused_computation.1 | loop fusion | flops 15360 | bytes 61444 | tf_op jit(solution)/shard_map/add | solution.py:301
  55.7 0.0 copy-done
  55.7 1.4 %multiply_add_fusion = f32[2,8,512]{2,1,0:T(8,128)} fusion(f32[2,8,512]{2,1,0:T(8,128)} %get-tuple-element.4, f32[2,8,512]{2,1,0:T(8,128)S(1)} %copy-done), kind=kLoop, calls=%fused_computation | loop fusion | flops 24576 | bytes 98304 | tf_op jit(solution)/shard_map/add | solution.py:300
Async XLA Ops:
  0.6 53.6 %copy-start.1 = (f32[5,4,256]{2,1,0:T(4,128)S(1)}, f32[5,4,256]{2,1,0:T(4,128)}, u32[]{:S(2)}) copy-start(f32[5,4,256]{2,1,0:T(4,128)} %param.7) | copy-start | bytes 61444
  0.7 55.0 %copy-start = (f32[2,8,512]{2,1,0:T(8,128)S(1)}, f32[2,8,512]{2,1,0:T(8,128)}, u32[]{:S(2)}) copy-start(f32[2,8,512]{2,1,0:T(8,128)} %param.6) | copy-start | bytes 98308
